TPU v7x, 32 devices: a whole 2x2x4 slice. The times are simulated.
32 devices in a mesh: groups: 2 (over x), ctx: 16 (over z, y, core).
Axes of the slice: x: 2, y: 2, z: 4, core: 2. Of those that a mesh axis runs over, the one named last changes fastest.
Arguments:
- patches: bfloat16 [128, 3200], P(('groups', 'ctx')), parts along dimension 0, may hold values from -60 to 60
- vit_gain: float32 [3200], replicated, may hold values from 0.1 to 1.9
- vit_fc1: bfloat16 [3200, 12800], P(None, 'ctx'), may hold values from -0.109375 to 0.109375
- vit_fc2: bfloat16 [12800, 3200], P('ctx'), may hold values from -0.0546875 to 0.0546875
- proj_gain: float32 [12800], replicated, may hold values from 0.1 to 1.9
- proj_bias: float32 [12800], replicated, may hold values from -3 to 3
- proj_weight: bfloat16 [12800, 8192], P(None, 'ctx'), may hold values from -0.0546875 to 0.0546875
- llm_gain: float32 [8192], P('ctx'), may hold values from 0.1 to 1.9
- qkv_weight: bfloat16 [8192, 10240], P('ctx'), may hold values from -0.0625 to 0.0625
- text_query: bfloat16 [2048, 8192], P(('groups', 'ctx')), parts along dimension 0, may hold values from -130 to 130
- text_keyvalue: bfloat16 [2048, 2048], P(('groups', 'ctx')), parts along dimension 0, may hold values from -6 to 6
- doc_ids: int32 [2048], P(('groups', 'ctx')), parts along dimension 0, may hold values from 0 to 3, never falling along the last dimension, each value on 1 to 640 neighbouring positions
- image_positions: int32 [32], P('groups'), parts along dimension 0, may hold values from 0 to 1023, as said below
Outputs:
- attended: bfloat16 [2048, 8192], P(('groups', 'ctx')), parts along dimension 0
There are 2 independent parts, one for each index of `groups`. A program takes and returns all parts, laid end to end along the dimension named above; an argument that names none is the same for every part. Nothing has to cross between parts.
Inputs may be any that keep to these rules, and one draw needn't show every extreme that they name: `image_positions`: strictly increasing; of the 64 positions of one shard (starting at a multiple of 64) at most 2 hold image tokens, and some shard holds exactly 2.
All inputs are finite; a program needn't handle non-finite values.
Results may differ from a plain program's by a relative error of at most 0.0044.
Values may be sent and summed in bfloat16 or wider, within the bound.
A program may use at most 192 MiB of HBM per device.

v0:
```python
import jax
import jax.numpy as jnp
from jax import lax
from jax.sharding import PartitionSpec as P

DV = 3200
SHUF = 4
D = 8192
QH = 64
KVH = 8
HD = 128
CAP = 2


def rotate(rows, positions):
    row_count = rows.shape[0]
    half_dim = HD // 2
    inv_freq = 1000000.0 ** (-2.0 * jnp.arange(half_dim, dtype=jnp.float32) / HD)
    angles = positions.astype(jnp.float32)[:, None] * inv_freq[None, :]
    cosine = jnp.cos(angles)[:, None, :]
    sine_part = jnp.sin(angles)[:, None, :]

    def rotate_part(part, head_count):
        head_grid = part.reshape(row_count, head_count, HD)
        lower = head_grid[..., :half_dim]
        upper = head_grid[..., half_dim:]
        turned = jnp.concatenate(
            [lower * cosine - upper * sine_part, upper * cosine + lower * sine_part], axis=-1
        )
        return turned.reshape(row_count, head_count * HD)

    query_part = rotate_part(rows[:, : QH * HD], QH)
    key_part = rotate_part(rows[:, QH * HD : (QH + KVH) * HD], KVH)
    return jnp.concatenate([query_part, key_part, rows[:, (QH + KVH) * HD :]], axis=1)


def attend_block(running, query_grid, key_block, key_pos, key_doc, query_pos, query_doc, scale):
    row_max, denom, context_sum = running
    key_rows = key_block[:, 0]
    value_rows = key_block[:, 1]
    scores = (
        jnp.einsum("qgmd,kgd->gmqk", query_grid, key_rows, preferred_element_type=jnp.float32)
        * scale
    )
    allowed = (key_pos[None, :] <= query_pos[:, None]) & (key_doc[None, :] == query_doc[:, None])
    scores = jnp.where(allowed, scores, -1e30)
    new_max = jnp.maximum(row_max, jnp.max(scores, axis=-1))
    weights = jnp.where(allowed, jnp.exp(scores - new_max[..., None]), 0.0)
    rescale = jnp.exp(row_max - new_max)
    denom = denom * rescale + jnp.sum(weights, axis=-1)
    context = jnp.einsum(
        "gmqk,kgd->qgmd",
        weights.astype(jnp.bfloat16),
        value_rows,
        preferred_element_type=jnp.float32,
    )
    context_sum = context_sum * jnp.transpose(rescale, (2, 0, 1))[..., None] + context
    return (new_max, denom, context_sum)


def shards(
    patches,
    vit_gain,
    vit_fc1,
    vit_fc2,
    proj_gain,
    proj_bias,
    proj_weight,
    llm_gain,
    qkv_weight,
    text_query,
    text_keyvalue,
    doc_ids,
    image_positions,
):
    device_index = lax.axis_index("ctx")
    patch_rows = patches.shape[0]
    seq_rows = text_query.shape[0]
    image_total = image_positions.shape[0]
    group = QH // KVH
    scale = HD ** (-0.5)
    values = patches.astype(jnp.float32)
    vit_norm = (
        values * lax.rsqrt(jnp.mean(values * values, axis=-1, keepdims=True) + 1e-06) * vit_gain
    ).astype(jnp.bfloat16)
    vit_hidden = jax.nn.gelu(
        jnp.dot(
            lax.all_gather(vit_norm, "ctx", axis=0, tiled=True),
            vit_fc1,
            preferred_element_type=jnp.float32,
        ),
        approximate=False,
    ).astype(jnp.bfloat16)
    vit_out = (
        values
        + lax.psum_scatter(
            jnp.dot(vit_hidden, vit_fc2, preferred_element_type=jnp.float32),
            "ctx",
            scatter_dimension=0,
            tiled=True,
        )
    ).astype(jnp.bfloat16)
    shuffled = vit_out.reshape(patch_rows // SHUF, SHUF * DV).astype(jnp.float32)
    row_mean = jnp.mean(shuffled, axis=-1, keepdims=True)
    centre = shuffled - row_mean
    variance = jnp.mean(centre * centre, axis=-1, keepdims=True)
    proj_norm = (centre * lax.rsqrt(variance + 1e-05) * proj_gain + proj_bias).astype(jnp.bfloat16)
    projected = jax.nn.gelu(
        jnp.dot(
            lax.all_gather(proj_norm, "ctx", axis=0, tiled=True),
            proj_weight,
            preferred_element_type=jnp.float32,
        ),
        approximate=False,
    ).astype(jnp.bfloat16)
    proj_float = projected.astype(jnp.float32)
    squares = lax.psum(jnp.sum(proj_float * proj_float, axis=-1), "ctx")
    inv_rms = lax.rsqrt(squares / D + 1e-06)
    llm_norm = (proj_float * inv_rms[:, None] * llm_gain).astype(jnp.bfloat16)
    owner_shard = image_positions // seq_rows
    token_ids = jnp.arange(image_total, dtype=jnp.int32)
    earlier = jnp.sum((owner_shard[None, :] < owner_shard[:, None]).astype(jnp.int32), axis=1)
    target = owner_shard * CAP + token_ids - earlier
    slot_ids = jnp.arange(CAP * lax.axis_size("ctx"), dtype=jnp.int32)
    select = (slot_ids[:, None] == target[None, :]).astype(jnp.bfloat16)
    picked = jnp.dot(select, llm_norm, preferred_element_type=jnp.float32).astype(jnp.bfloat16)
    own_slots = lax.psum_scatter(
        jnp.dot(picked, qkv_weight, preferred_element_type=jnp.float32),
        "ctx",
        scatter_dimension=0,
        tiled=True,
    )
    my_slots = device_index * CAP + jnp.arange(CAP, dtype=jnp.int32)
    slot_hits = my_slots[:, None] == target[None, :]
    row_live = jnp.any(slot_hits, axis=1)
    row_pos = jnp.sum(jnp.where(slot_hits, image_positions[None, :], 0), axis=1)
    placed_rows = rotate(own_slots, row_pos).astype(jnp.bfloat16)
    local_row = row_pos - device_index * seq_rows
    insert = (jnp.arange(seq_rows, dtype=jnp.int32)[:, None] == local_row[None, :]) & row_live[
        None, :
    ]
    is_image = jnp.any(insert, axis=1)[:, None]
    insert_table = insert.astype(jnp.bfloat16)
    query = jnp.where(
        is_image,
        jnp.dot(insert_table, placed_rows[:, : QH * HD], preferred_element_type=jnp.float32).astype(
            jnp.bfloat16
        ),
        text_query,
    )
    keyvalue = jnp.where(
        is_image,
        jnp.dot(insert_table, placed_rows[:, QH * HD :], preferred_element_type=jnp.float32).astype(
            jnp.bfloat16
        ),
        text_keyvalue,
    )
    doc_all = lax.all_gather(doc_ids, "ctx", axis=0, tiled=True)
    query_pos = device_index * seq_rows + jnp.arange(seq_rows, dtype=jnp.int32)
    kv_grid = keyvalue.reshape(seq_rows, 2, KVH, HD)
    query_grid = query.reshape(seq_rows, KVH, group, HD)
    start_state = (
        jnp.full((KVH, group, seq_rows), -1e30, jnp.float32),
        jnp.zeros((KVH, group, seq_rows), jnp.float32),
        jnp.zeros((seq_rows, KVH, group, HD), jnp.float32),
    )
    running = start_state
    shard_rows = lax.all_gather(kv_grid, "ctx", axis=0, tiled=True)
    first_row = jnp.int32(0)
    row_total = shard_rows.shape[0]
    for offset in range(0, row_total, 512):
        block_size = min(512, row_total - offset)
        key_block = shard_rows[offset : offset + block_size]
        key_pos = first_row + offset + jnp.arange(block_size, dtype=jnp.int32)
        key_doc = lax.dynamic_slice_in_dim(doc_all, offset, block_size, 0)
        running = attend_block(
            running, query_grid, key_block, key_pos, key_doc, query_pos, doc_ids, scale
        )
    row_max, denom, context_sum = running
    attended = (context_sum / jnp.transpose(denom, (2, 0, 1))[..., None]).astype(jnp.bfloat16)
    return attended.reshape(seq_rows, QH * HD)


def solution(mesh):
    placed = (
        P(("groups", "ctx"), None),
        P(),
        P(None, "ctx"),
        P("ctx", None),
        P(),
        P(),
        P(None, "ctx"),
        P("ctx"),
        P("ctx", None),
        P(("groups", "ctx"), None),
        P(("groups", "ctx"), None),
        P(("groups", "ctx")),
        P("groups"),
    )
    return jax.shard_map(
        shards, mesh=mesh, in_specs=placed, out_specs=P(("groups", "ctx"), None), check_vma=False
    )
```

profile of v0, /device:TPU:1, one launch (start us, length us, event | category | flops | bytes accessed | tf_op | source)
XLA Modules:
  0.0 370.9 jit_solution(12137119046432978185)
XLA Ops:
  6.5 0.0 copy-start.6
  6.5 0.0 copy-start.8
  6.5 0.0 copy-start.4
  6.5 0.0 copy-start.3
  6.5 0.0 all-reduce.6.cloned.1.call-start
  6.6 0.9 fusion.75
  7.5 0.8 fusion.100
  8.4 24.1 %all-gather.1 = bf16[16,4,3200]{2,1,0:T(4,128)(2,1)S(1)} all-gather(bf16[1,4,3200]{2,1,0:T(4,128)(2,1)S(1)} %fusion.100), channel_id=1, replica_groups=mesh['groups'=2,'ctx'=16] {'ctx'}, dimensions={0}, use_global_device_ids=true | all-gather | bytes 435200 | tf_op jit(solution)/shard_map/all_gather | solution.py:88
  32.5 0.1 reshape.169
  32.6 8.5 %fusion.40 = f32[64,3200]{1,0:T(8,128)} fusion(bf16[800,3200]{1,0:T(8,128)(2,1)} %param.16, bf16[64,3200]{1,0:T(8,128)(2,1)S(1)} %reshape.169, bf16[3200,800]{0,1:T(8,128)(2,1)} %param.15), kind=kOutput, calls=%fused_computation.61 | convolution fusion | flops 658688000 | bytes 11468800 | tf_op jit(solution)/shard_map/dot_general | solution.py:97
  41.1 0.0 all-reduce.6.cloned.1.call-update
  41.1 0.0 all-reduce.8.cloned.1.call-start
  41.2 0.0 copy-done.8
  41.2 0.2 convert_reduce_fusion.1
  41.4 0.0 copy-done.6
  41.4 0.6 fusion.155
  43.3 0.2 compare_reduce_fusion
  43.5 0.2 fusion.112
  43.7 86.4 %all-reduce.6.cloned.1.call-done = f32[64,3200]{1,0:T(8,128)} async-done(((f32[64,3200]{1,0:T(8,128)}), f32[64,3200]{1,0:T(8,128)}) %all-reduce.6.cloned.1.call-update) | async-done | bytes 819216
  130.1 0.0 copy-done.2
  130.1 1.5 convert_reduce_fusion
  132.3 0.6 fusion.74
  133.7 0.0 copy-done.4
  133.7 0.0 copy-done.3
  133.7 23.2 %all-gather.2 = bf16[16,1,12800]{2,1,0:T(2,128)(2,1)S(1)} all-gather(bf16[1,1,12800]{2,1,0:T(2,128)(2,1)S(1)} %reshape.170), channel_id=2, replica_groups=mesh['groups'=2,'ctx'=16] {'ctx'}, dimensions={0}, use_global_device_ids=true | all-gather | bytes 435200 | tf_op jit(solution)/shard_map/all_gather | solution.py:110
  156.9 6.7 %fusion.79 = (f32[16]{0:T(128)S(1)}, bf16[16,512]{1,0:T(8,128)(2,1)S(1)}) fusion(bf16[12800,512]{1,0:T(8,128)(2,1)} %param.19, bf16[16,1,12800]{2,1,0:T(2,128)(2,1)S(1)} %all-gather.2), kind=kOutput, calls=%fused_computation.113 | convolution fusion | flops 210272240 | bytes 13533248 | tf_op jit(solution)/shard_map/dot_general | solution.py:109
  163.6 0.0 copy-start.1
  163.7 0.0 copy-start.7
  163.7 0.0 copy-start
  163.7 29.1 %psum.7 = f32[16]{0:T(128)S(1)} all-reduce(f32[16]{0:T(128)S(1)} %get-tuple-element.26), channel_id=1, replica_groups=mesh['groups'=2,'ctx'=16] {'ctx'}, use_global_device_ids=true, to_apply=%region_9.10 | all-reduce | flops 16 | bytes 128 | tf_op jit(solution)/shard_map/psum | solution.py:117
  192.8 0.0 copy-done.5
  192.8 7.1 %fusion.21 = f32[32,10240]{1,0:T(8,128)} fusion(bf16[512,10240]{1,0:T(8,128)(2,1)} %param.21, bf16[16,512]{1,0:T(8,128)(2,1)S(1)} %get-tuple-element.27, f32[512]{0:T(512)S(1)} %copy-done.5, f32[16]{0:T(128)S(1)} %add_rsqrt_fusion, s32[16]{0:T(128)S(1)} %add_subtract_fusion), kind=kOutput, calls=%fused_computation.26 | convolution fusion | flops 336118272 | bytes 11815040 | tf_op jit(solution)/shard_map/dot_general | solution.py:128
  200.0 0.0 all-reduce.8.cloned.1.call-update
  200.0 0.0 all-gather.5.cloned.1.call-start
  200.1 0.1 fusion.150
  200.1 0.1 multiply_cosine_fusion
  200.3 91.0 %all-reduce.8.cloned.1.call-done = f32[32,10240]{1,0:T(8,128)} async-done(((f32[32,10240]{1,0:T(8,128)}), f32[32,10240]{1,0:T(8,128)}) %all-reduce.8.cloned.1.call-update) | async-done | bytes 1310736
  291.2 0.8 dynamic-slice_bitcast_fusion.1
  292.1 0.1 subtract_convert_fusion.1
  292.2 0.1 maximum_bitcast_fusion.1
  292.3 0.8 dynamic-slice.12
  293.1 0.0 copy-done.1
  293.1 0.4 fusion.20
  293.5 0.8 copy.25
  294.3 0.0 all-gather.5.cloned.1.call-update
  294.9 0.0 copy-done.7
  294.9 0.2 dynamic-update-slice
  295.1 8.5 %all-reduce = s32[1024]{0:T(1024)S(1)} all-reduce(s32[1024]{0:T(1024)S(1)} %dynamic-update-slice), channel_id=1, replica_groups=mesh['groups'=2,'ctx'=16] {'ctx'}, use_global_device_ids=true, to_apply=%add | all-reduce | flops 1024 | bytes 8192
  303.6 0.1 fusion.39
  303.8 1.0 dynamic-slice_bitcast_fusion
  304.8 0.1 subtract_convert_fusion
  304.9 0.1 maximum_bitcast_fusion
  305.0 0.0 copy-done
  305.0 0.6 fusion.19
  305.6 0.3 copy.39
  305.8 39.7 %all-gather.5.cloned.1.call-done = bf16[1024,2,8,128]{3,0,2,1:T(8,128)(2,1)} async-done(((bf16[64,2,8,128]{3,0,2,1:T(8,128)(2,1)}), bf16[1024,2,8,128]{3,0,2,1:T(8,128)(2,1)}) %all-gather.5.cloned.1.call-update) | async-done | bytes 4194320 | tf_op jit(solution)/shard_map/all_gather | solution.py:168
  345.5 3.4 fusion.1
  348.9 0.0 copy-done.9
  349.0 2.1 fusion.2
  351.1 5.3 %fusion.3 = (f32[8,8,64]{2,1,0:T(8,128)S(1)}, f32[8,8,64]{2,1,0:T(8,128)S(1)}) fusion(f32[8,512,64,8]{1,2,3,0:T(8,128)S(1)} %get-tuple-element.29, f32[8,8,64]{2,1,0:T(8,128)S(1)} %get-tuple-element.12, pred[64,512]{1,0:T(8,128)(4,1)S(1)} %get-tuple-element.18, f32[8,8,64]{2,1,0:T(8,128)S(1)} %get-tuple-element.13, ...), kind=kLoop, calls=%fused_computation.8 | loop fusion | flops 20963328 | bytes 16908288 | tf_op jit(solution)/shard_map/reduce_sum | solution.py:50
  356.4 2.1 fusion.7
  358.6 3.4 fusion.15
  362.0 0.7 copy.28
  362.7 1.7 copy.65
  (24 shorter events, 0.2 us)
Async XLA Ops:
  6.5 34.8 %copy-start.6 = (u32[32]{0:T(128)S(1)}, u32[32]{0:T(128)}, u32[]{:S(2)}) copy-start(u32[32]{0:T(128)} %constant.35) | copy-start | bytes 388
  6.5 123.6 %copy-start.2 = (bf16[4,3200]{1,0:T(4,128)(2,1)S(1)}, bf16[4,3200]{1,0:T(4,128)(2,1)}, u32[]{:S(2)}) copy-start(bf16[4,3200]{1,0:T(4,128)(2,1)} %param.13) | copy-start | bytes 76804
  6.5 34.6 %copy-start.8 = (s32[16]{0:T(128)S(1)}, s32[16]{0:T(128)}, u32[]{:S(2)}) copy-start(s32[16]{0:T(128)} %param.25) | copy-start | bytes 196
  6.5 127.1 %copy-start.4 = (f32[12800]{0:T(1024)S(1)}, f32[12800]{0:T(1024)}, u32[]{:S(2)}) copy-start(f32[12800]{0:T(1024)} %param.17) | copy-start | bytes 153604
  6.5 127.1 %copy-start.3 = (f32[12800]{0:T(1024)S(1)}, f32[12800]{0:T(1024)}, u32[]{:S(2)}) copy-start(f32[12800]{0:T(1024)} %param.18) | copy-start | bytes 153604
  6.5 123.6 %all-reduce.6.cloned.1.call-start = ((), (), s32[]{:S(2)}) async-start(), calls=%async_computation.1 | async-start | bytes 1638400
  41.1 250.1 %all-reduce.8.cloned.1.call-start = ((), (), s32[]{:S(2)}) async-start(), calls=%async_computation.2 | async-start | bytes 2621440
  156.9 35.9 %copy-start.5 = (f32[512]{0:T(512)S(1)}, f32[512]{0:T(512)}, u32[]{:S(2)}) copy-start(f32[512]{0:T(512)} %param.20) | copy-start | bytes 6148
  163.6 129.5 %copy-start.1 = (bf16[64,2048]{1,0:T(8,128)(2,1)S(1)}, bf16[64,2048]{1,0:T(8,128)(2,1)}, u32[]{:S(2)}) copy-start(bf16[64,2048]{1,0:T(8,128)(2,1)} %param.23) | copy-start | bytes 786436
  163.7 131.2 %copy-start.7 = (s32[64]{0:T(128)S(1)}, s32[64]{0:T(128)}, u32[]{:S(2)}) copy-start(s32[64]{0:T(128)} %param.24) | copy-start | bytes 772
  163.7 141.3 %copy-start = (bf16[64,8192]{1,0:T(8,128)(2,1)S(1)}, bf16[64,8192]{1,0:T(8,128)(2,1)}, u32[]{:S(2)}) copy-start(bf16[64,8192]{1,0:T(8,128)(2,1)} %param.22) | copy-start | bytes 3145732
  200.0 145.5 %all-gather.5.cloned.1.call-start = ((), (), s32[]{:S(2)}) async-start(), calls=%async_computation | async-start | bytes 4456448 | tf_op jit(solution)/shard_map/all_gather | solution.py:168
  345.5 3.4 copy-start.9
Sparse Core Ops, SparseCore 0:
  41.2 88.8 all-reduce.5
  200.1 91.0 all-reduce.7
  294.4 51.0 all-gather.4
where the time goes:
time: 372 us; the launch traced here: 371 us
  waiting for transfers between devices  217 us (58%)
  blocking collectives  84.9 us (23%)
  matrix products  34.4 us (9%)
  between operations  16.6 us (4%)
  other arithmetic  10.6 us (3%)
  local copies, waits for them, and re-layouts  7.19 us (2%)
    unnamed x5, waiting for transfers between devices  177 us
    all_gather x1, waiting for transfers between devices, shards(): shard_rows = lax.all_gather(kv_grid, 'ctx', axis=0, tiled=True)  39.7 us
    psum x1, blocking collectives, shards(): squares = lax.psum(jnp.sum(proj_float * proj_float, axis=-1), 'ctx')  29.1 us
    all_gather x1, blocking collectives, shards(): lax.all_gather(vit_norm, 'ctx', axis=0, tiled=True)  24.1 us
    all_gather x1, blocking collectives, shards(): lax.all_gather(proj_norm, 'ctx', axis=0, tiled=True)  23.2 us
    dot_general x1, matrix products, shards(): jnp.dot(vit_hidden, vit_fc2, preferred_element_type=jnp.float32)  8.51 us
    unnamed x1, blocking collectives  8.5 us
  transfers between devices with their start and end apart: 3, of which 3 were waited for; matrix products, arithmetic and copies ran while one was open for 1% of the time, Pallas kernels for 0%

commit v1 on v0

v1 whole, which is shorter than its diff:
```python
import functools
import jax
import jax.numpy as jnp
from jax import lax
from jax.experimental import pallas as pl
from jax.experimental.pallas import tpu as pltpu
from jax.sharding import PartitionSpec as P

DV = 3200
SHUF = 4
D = 8192
QH = 64
KVH = 8
HD = 128
ROWW = 2560
EXT = 128
F32 = jnp.float32
BF16 = jnp.bfloat16


def gelu(x):
    return 0.5 * x * (1.0 + lax.erf(x * (2.0 ** -0.5)))


def narrow_plain(dst, v):
    dst[...] = v.astype(BF16)


def two_parts(total):
    lane = lax.broadcasted_iota(jnp.int32, (total.shape[0], EXT), 1)
    high = total.astype(BF16).astype(F32)
    return jnp.where(lane == 0, high, jnp.where(lane == 1, total - high, 0.0))


def narrow_ext(dst, v):
    dst[:, :ROWW] = v[:, :ROWW].astype(BF16)
    dst[:, ROWW:] = two_parts(jnp.sum(v[:, ROWW:], axis=1, keepdims=True)).astype(BF16)


def image_kernel(
    n,
    patches,
    vit_gain,
    fc1_hbm,
    fc2_hbm,
    proj_gain,
    proj_bias,
    proj_hbm,
    llm_gain,
    qkv_hbm,
    turn,
    out,
    fc1,
    fc2,
    proj,
    qkv,
    g1, g2, g3,
    b1, r1a, a1b, r1b, a1c, r1c,
    b2, r2a, a2b, r2b, a2c, r2c,
    work,
    lhs,
    hid_acc,
    hidden,
    proj_acc,
    wsem,
    ag_send, ag_recv,
    rs_send, rs_recv,
):
    Z = n // 4
    group = lax.axis_index("groups")
    me = lax.axis_index("ctx")
    z, y, c = me // 4, lax.rem(me // 2, 2), lax.rem(me, 2)

    def dev(zz, yy, cc):
        return (group, zz * 4 + yy * 2 + cc)

    zs = [lax.rem(z + k, Z) for k in range(Z)]
    zr = [lax.rem(z + Z - k, Z) for k in range(Z)]
    ydev, cdev = dev(z, 1 - y, c), dev(z, y, 1 - c)
    own = (c * 2 + y) * Z
    own_y = (c * 2 + 1 - y) * Z
    slot = own + z

    loads = [pltpu.make_async_copy(fc1_hbm, fc1, wsem.at[0]),
             pltpu.make_async_copy(fc2_hbm, fc2, wsem.at[1])]
    for r in range(SHUF):
        loads.append(pltpu.make_async_copy(
            proj_hbm.at[pl.ds(r * DV, DV)], proj.at[pl.ds(r * DV, DV)], wsem.at[2 + r]))
    loads.append(pltpu.make_async_copy(qkv_hbm, qkv, wsem.at[2 + SHUF]))
    for load in loads:
        load.start()

    barrier = pltpu.get_barrier_semaphore()
    partners = [dev(zs[k], y, c) for k in range(1, Z)] + [ydev, cdev]
    for partner in partners:
        pl.semaphore_signal(barrier, inc=1, device_id=partner, device_id_type=pl.DeviceIdType.MESH)
    pl.semaphore_wait(barrier, len(partners))

    def remote(src, dst, ss, rs, to):
        return pltpu.make_async_remote_copy(
            src_ref=src, dst_ref=dst, send_sem=ss, recv_sem=rs,
            device_id=to, device_id_type=pl.DeviceIdType.MESH)

    def gather(buf, which):
        ss, rs = ag_send.at[which], ag_recv.at[which]
        sent = []

        def send(at, sem, to):
            copy = remote(buf.at[at], buf.at[at], ss.at[sem], rs.at[sem], to)
            copy.start()
            sent.append(copy)

        def arrived(at, sem):
            remote(buf.at[at], buf.at[at], ss.at[sem], rs.at[sem], cdev).wait_recv()

        for k in range(1, Z):
            send(slot, k, dev(zs[k], y, c))
        send(slot, Z, ydev)
        send(slot, 2 * Z, cdev)
        for k in range(1, Z):
            arrived(own + zr[k], k)
            send(own + zr[k], Z + k, ydev)
            send(own + zr[k], 2 * Z + k, cdev)
        for k in range(Z):
            arrived(own_y + zr[k], Z + k)
            send(own_y + zr[k], 3 * Z + k, cdev)
        other = ((1 - c) * 2 + y) * Z
        other_y = ((1 - c) * 2 + 1 - y) * Z
        for k in range(Z):
            arrived(other + zr[k], 2 * Z + k)
        for k in range(Z):
            arrived(other_y + zr[k], 3 * Z + k)
        return sent

    def reduce(buf, ra, ab, rb, ac, rc, which, narrow):
        ss, rs = rs_send.at[which], rs_recv.at[which]
        sent = []

        def send(src, dst, sem, to):
            copy = remote(src, dst, ss.at[sem], rs.at[sem], to)
            copy.start()
            sent.append(copy)

        def arrived(dst, sem):
            remote(dst, dst, ss.at[sem], rs.at[sem], cdev).wait_recv()

        for half in range(2):
            yy = (1 - y) if half == 0 else y
            send(buf.at[pl.ds(((1 - c) * 2 + yy) * Z, Z)], ra.at[half], half, cdev)
        arrived(ra.at[0], 0)
        order = list(range(1, Z)) + [0]
        for k in order:
            narrow(ab.at[k], buf[own_y + zs[k]].astype(F32) + ra[0, zs[k]].astype(F32))
            send(ab.at[k], rb.at[k], 2 + k, ydev)
        arrived(ra.at[1], 1)
        total = None
        for k in order:
            arrived(rb.at[k], 2 + k)
            mine = (buf[own + zs[k]].astype(F32) + ra[1, zs[k]].astype(F32)) + rb[k].astype(F32)
            if k == 0:
                total = mine
            else:
                narrow(ac.at[k], mine)
                send(ac.at[k], rc.at[k], Z + 2 + k, dev(zs[k], y, c))
        for k in range(1, Z):
            arrived(rc.at[k], Z + 2 + k)
            total = total + rc[k].astype(F32)
        return total, sent

    def unpack(buf, width, place=lambda i: i):
        for i in range(n):
            v = buf[i].astype(F32)
            for j in range(width // 128):
                work[j, pl.ds(4 * place(i), 4), :] = v[:, j * 128:(j + 1) * 128]

    def pack(buf, width):
        for i in range(n):
            for j in range(width // 128):
                buf[i, :, pl.ds(j * 128, 128)] = work[j, pl.ds(4 * i, 4), :].astype(BF16)

    values = patches[...].astype(F32)
    mean_sq = jnp.mean(values * values, axis=-1, keepdims=True)
    g1[slot] = (values * lax.rsqrt(mean_sq + 1e-6) * vit_gain[...]).astype(BF16)
    sends = gather(g1, 0)

    unpack(g1, DV)
    for j in range(DV // 128):
        lhs[:, pl.ds(j * 128, 128)] = work[j].astype(BF16)
    loads[0].wait()
    hid_acc[...] = jnp.zeros_like(hid_acc)

    @pl.loop(0, DV // 640)
    def _(j):
        at = pl.ds(pl.multiple_of(j * 640, 128), 640)
        hid_acc[...] += jnp.dot(lhs[:, at], fc1[at, :], preferred_element_type=F32)

    hidden[...] = gelu(hid_acc[...]).astype(BF16)
    loads[1].wait()

    @pl.loop(0, DV // 640)
    def _(j):
        at = pl.ds(pl.multiple_of(j * 640, 128), 640)
        part = jnp.dot(hidden[...], fc2[:, at], preferred_element_type=F32)
        for m in range(5):
            work[j * 5 + m] = part[:, m * 128:(m + 1) * 128]

    pack(b1, DV)
    total, more = reduce(b1, r1a, a1b, r1b, a1c, r1c, 0, narrow_plain)
    sends += more
    shuffled = (patches[...].astype(F32) + total).astype(BF16).astype(F32)
    row_mean = jnp.sum(jnp.sum(shuffled, axis=1, keepdims=True), axis=0, keepdims=True) / (SHUF * DV)
    centre = shuffled - row_mean
    var = jnp.sum(jnp.sum(centre * centre, axis=1, keepdims=True), axis=0, keepdims=True) / (SHUF * DV)
    g2[slot] = (centre * lax.rsqrt(var + 1e-5) * proj_gain[...] + proj_bias[...]).astype(BF16)
    sends += gather(g2, 1)

    unpack(g2, DV)
    proj_acc[...] = jnp.zeros_like(proj_acc)
    for r in range(SHUF):
        loads[2 + r].wait()
        lhs[:n, :] = jnp.concatenate(
            [work[j, pl.ds(r, n, stride=4), :] for j in range(DV // 128)], axis=1
        ).astype(BF16)

        @pl.loop(0, DV // 640)
        def _(j):
            at = pl.ds(pl.multiple_of(j * 640, 128), 640)
            rows = pl.ds(pl.multiple_of(r * DV + j * 640, 128), 640)
            proj_acc[...] += jnp.dot(lhs[:n, at], proj[rows, :], preferred_element_type=F32)

    projected = gelu(proj_acc[...]).astype(BF16).astype(F32)
    squares = two_parts(jnp.sum(projected * projected, axis=1, keepdims=True))
    scaled = (projected * llm_gain[...]).astype(BF16)
    loads[2 + SHUF].wait()
    for r in range(SHUF):
        for j in range(ROWW // 640):
            part = jnp.dot(scaled, qkv[:, pl.ds(r * ROWW + j * 640, 640)], preferred_element_type=F32)
            for m in range(5):
                work[j * 5 + m, pl.ds(r, n, stride=4), :] = part[:, m * 128:(m + 1) * 128]
        work[ROWW // 128, pl.ds(r, n, stride=4), :] = squares
    pack(b2, ROWW + EXT)
    total, more = reduce(b2, r2a, a2b, r2b, a2c, r2c, 1, narrow_ext)
    sends += more
    square_sum = jnp.sum(total[:, ROWW:], axis=1, keepdims=True)
    inv_rms = lax.rsqrt(square_sum / D + 1e-6)
    cosine, sine = turn[0:1, :], turn[1:2, :]
    row = lax.broadcasted_iota(jnp.int32, (SHUF, HD), 0)
    for h in range(ROWW // HD):
        x = total[:, h * HD:(h + 1) * HD] * inv_rms
        turned = x * cosine + pltpu.roll(x, HD // 2, 1) * sine
        g3[slot, :, pl.ds(h * HD, HD)] = jnp.where(
            row * (ROWW // HD) + h < QH + KVH, turned, x).astype(BF16)
    sends += gather(g3, 2)
    unpack(g3, ROWW, lambda i: (i % Z) * 4 + (i // Z) % 2 * 2 + i // (2 * Z))
    for r in range(SHUF):
        for j in range(ROWW // HD):
            out[:, pl.ds(r * ROWW + j * HD, HD)] = work[j, pl.ds(r, n, stride=4), :].astype(BF16)
    for copy in sends:
        copy.wait_send()


def image_rows(n, patches, vit_gain, fc1, fc2, proj_gain, proj_bias, proj, llm_gain, qkv, turn):
    Z = n // 4
    vm = pl.BlockSpec(memory_space=pltpu.VMEM)
    hbm = pl.BlockSpec(memory_space=pl.ANY)

    def reduce_bufs(width):
        return [
            pltpu.VMEM((n, SHUF, width), BF16),
            pltpu.VMEM((2, Z, SHUF, width), BF16),
        ] + [pltpu.VMEM((Z, SHUF, width), BF16)] * 4

    hid = fc1.shape[1]
    cols = proj.shape[1]
    weights = sum(w.size for w in (fc1, fc2, proj, qkv))
    return pl.pallas_call(
        functools.partial(image_kernel, n),
        out_shape=jax.ShapeDtypeStruct((n, SHUF * ROWW), BF16),
        in_specs=[vm, vm, hbm, hbm, vm, vm, hbm, vm, hbm, vm],
        out_specs=vm,
        scratch_shapes=[
            pltpu.VMEM(fc1.shape, BF16),
            pltpu.VMEM(fc2.shape, BF16),
            pltpu.VMEM(proj.shape, BF16),
            pltpu.VMEM(qkv.shape, BF16),
            pltpu.VMEM((n, SHUF, DV), BF16),
            pltpu.VMEM((n, SHUF, DV), BF16),
            pltpu.VMEM((n, SHUF, ROWW), BF16),
        ] + reduce_bufs(DV) + reduce_bufs(ROWW + EXT) + [
            pltpu.VMEM((DV // 128, n * SHUF, 128), F32),
            pltpu.VMEM((n * SHUF, DV), BF16),
            pltpu.VMEM((n * SHUF, hid), F32),
            pltpu.VMEM((n * SHUF, hid), BF16),
            pltpu.VMEM((n, cols), F32),
            pltpu.SemaphoreType.DMA((3 + SHUF,)),
            pltpu.SemaphoreType.DMA((3, 4 * Z)),
            pltpu.SemaphoreType.DMA((3, 4 * Z)),
            pltpu.SemaphoreType.DMA((2, 2 * Z + 2)),
            pltpu.SemaphoreType.DMA((2, 2 * Z + 2)),
        ],
        compiler_params=pltpu.CompilerParams(
            collective_id=0, has_side_effects=True, vmem_limit_bytes=56 * 2 ** 20),
        cost_estimate=pl.CostEstimate(
            flops=64 * weights, bytes_accessed=2 * weights, transcendentals=0),
    )(patches, vit_gain, fc1, fc2, proj_gain, proj_bias, proj, llm_gain, qkv, turn)


def attend_kernel(n, span, width, query, keys, vals, doc, pos, iq, ik, iv, out, bias, hit_k, img_k, hit_q, img_q):
    rows = query.shape[0]
    me = lax.axis_index("ctx")
    first = jnp.clip(lax.div(jnp.maximum(me - span, 0), 2) * 2, 0, n - width // rows) * rows
    first = pl.multiple_of(first, 2 * rows)
    group = QH // KVH

    @pl.when(pl.program_id(0) == 0)
    def _():
        docs = doc[...]
        q_pos = me * rows + lax.broadcasted_iota(jnp.int32, (rows, docs.shape[1]), 0)
        k_pos = lax.broadcasted_iota(jnp.int32, (rows, docs.shape[1]), 1)
        q_doc = jnp.sum(jnp.where(q_pos == k_pos, docs, 0), axis=1, keepdims=True)
        k_doc = doc[:, pl.ds(first, width)]
        ok = (first + k_pos[:, :width] <= q_pos[:, :width]) & (k_doc == q_doc)
        bias[...] = jnp.where(ok, 0.0, -1e30)

        def hits(count, start):
            at = start + lax.broadcasted_iota(jnp.int32, (count, n), 0)
            hit = (at == pos[...]).astype(F32)
            return hit.astype(BF16), jnp.sum(hit, axis=1, keepdims=True)

        table, live = hits(width, first)
        hit_k[...] = table
        img_k[...] = jnp.broadcast_to(live, img_k.shape)
        table, live = hits(rows, me * rows)
        hit_q[...] = table
        img_q[...] = jnp.broadcast_to(live, img_q.shape)

    def put(live, table, image, text):
        placed = jnp.dot(table, image, preferred_element_type=F32)
        return jnp.where(live > 0.0, placed, text.astype(F32)).astype(BF16)

    k = put(img_k[...], hit_k[...], ik[...], keys[pl.ds(first, width), :])
    v = put(img_k[...], hit_k[...], iv[...], vals[pl.ds(first, width), :])
    scale = HD ** -0.5
    for m in range(group):
        at = slice(m * HD, (m + 1) * HD)
        q = put(img_q[...], hit_q[...], iq[:, at], query[:, at])
        s = lax.dot_general(q, k, (((1,), (1,)), ((), ())), preferred_element_type=F32)
        s = s * scale + bias[...]
        w = jnp.exp(s - jnp.max(s, axis=1, keepdims=True))
        total = jnp.sum(w, axis=1, keepdims=True)
        o = jnp.dot(w.astype(BF16), v, preferred_element_type=F32)
        out[:, at] = (o / total).astype(BF16)


def attention(n, query, keyvalue, doc, pos, image):
    rows = query.shape[0]
    seq = keyvalue.shape[0]
    group = QH // KVH
    span = seq * 5 // 8 // rows
    width = min(span + 2, n) * rows
    return pl.pallas_call(
        functools.partial(attend_kernel, n, span, width),
        grid=(KVH,),
        out_shape=jax.ShapeDtypeStruct((rows, QH * HD), BF16),
        in_specs=[
            pl.BlockSpec((rows, group * HD), lambda g: (0, g)),
            pl.BlockSpec((seq, HD), lambda g: (0, g)),
            pl.BlockSpec((seq, HD), lambda g: (0, KVH + g)),
            pl.BlockSpec((1, seq), lambda g: (0, 0)),
            pl.BlockSpec((1, n), lambda g: (0, 0)),
            pl.BlockSpec((n, group * HD), lambda g: (0, g)),
            pl.BlockSpec((n, HD), lambda g: (0, QH + g)),
            pl.BlockSpec((n, HD), lambda g: (0, QH + KVH + g)),
        ],
        out_specs=pl.BlockSpec((rows, group * HD), lambda g: (0, g)),
        scratch_shapes=[
            pltpu.VMEM((rows, width), F32),
            pltpu.VMEM((width, n), BF16),
            pltpu.VMEM((width, HD), F32),
            pltpu.VMEM((rows, n), BF16),
            pltpu.VMEM((rows, HD), F32),
        ],
        compiler_params=pltpu.CompilerParams(vmem_limit_bytes=48 * 2 ** 20),
        cost_estimate=pl.CostEstimate(
            flops=4 * rows * QH * HD * width, bytes_accessed=4 * query.size + 2 * keyvalue.size,
            transcendentals=rows * QH * width),
    )(query, keyvalue, keyvalue, doc, pos, image, image, image)


def shards(
    n,
    patches,
    vit_gain,
    vit_fc1,
    vit_fc2,
    proj_gain,
    proj_bias,
    proj_weight,
    llm_gain,
    qkv_weight,
    text_query,
    text_keyvalue,
    doc_ids,
    image_positions,
):
    kv_all = lax.all_gather(text_keyvalue, "ctx", axis=0, tiled=True)
    doc_all = lax.all_gather(doc_ids, "ctx", axis=0, tiled=True)
    half = HD // 2
    inv_freq = 1000000.0 ** (-2.0 * jnp.arange(half, dtype=F32) / HD)
    own_pos = lax.dynamic_index_in_dim(image_positions, lax.axis_index("ctx"), 0, keepdims=False)
    angle = own_pos.astype(F32) * inv_freq
    cosine, sine = jnp.cos(angle), jnp.sin(angle)
    turn = jnp.stack([jnp.concatenate([cosine, cosine]), jnp.concatenate([-sine, sine])])
    image = image_rows(
        n, patches, vit_gain.reshape(1, DV), vit_fc1, vit_fc2,
        proj_gain.reshape(SHUF, DV), proj_bias.reshape(SHUF, DV), proj_weight,
        llm_gain.reshape(1, -1), qkv_weight, turn)
    return attention(
        n, text_query, kv_all, doc_all.reshape(1, -1), image_positions.reshape(1, -1), image)


def solution(mesh):
    placed = (
        P(("groups", "ctx"), None),
        P(),
        P(None, "ctx"),
        P("ctx", None),
        P(),
        P(),
        P(None, "ctx"),
        P("ctx"),
        P("ctx", None),
        P(("groups", "ctx"), None),
        P(("groups", "ctx"), None),
        P(("groups", "ctx")),
        P("groups"),
    )
    return jax.shard_map(
        functools.partial(shards, mesh.shape["ctx"]), mesh=mesh, in_specs=placed,
        out_specs=P(("groups", "ctx"), None), check_vma=False)
```

time: 372 us -> 137 us (0.37)
  waiting for transfers between devices: 217 us -> 0.7 us
  Pallas kernels: 0 us -> 92.2 us
  blocking collectives: 84.9 us -> 11.9 us
  matrix products: 34.4 us -> 0 us
  other arithmetic: 10.6 us -> 0.84 us
  local copies, waits for them, and re-layouts: 7.19 us -> 15.8 us
    unnamed x5 -> x1, waiting for transfers between devices: 177 us -> 0.68 us
    pallas_call x0 -> x2, Pallas kernels: none -> 92.2 us  [the longest x1 61.2 us: image_rows(): pl.pallas_call(functools.partial(image_kernel, n), out_shape=jax.ShapeDty...]
    all_gather x2 -> x0, blocking collectives: 47.3 us -> none  [the longest x1 24.1 us: shards(): lax.all_gather(vit_norm, 'ctx', axis=0, tiled=True)]
    all_gather x1, waiting for transfers between devices: 39.7 us -> 0.02 us  [shards(): kv_all = lax.all_gather(text_keyvalue, 'ctx', axis=0, tiled=True)]
    dot_general x9 -> x0, matrix products: 34.4 us -> none  [the longest x1 8.51 us: shards(): jnp.dot(vit_hidden, vit_fc2, preferred_element_type=jnp.float32)]
    psum x1 -> x0, blocking collectives: 29.1 us -> none  [shards(): squares = lax.psum(jnp.sum(proj_float * proj_float, axis=-1), 'ctx')]
    reduce_sum x6 -> x0, other arithmetic: 8.77 us -> none  [the longest x1 5.33 us: attend_block(): denom = denom * rescale + jnp.sum(weights, axis=-1)]
    unnamed x33 -> x22, local copies, waits for them, and re-layouts: 4.87 us -> 12.7 us
  transfers between devices with their start and end apart: 3 -> 1, of which waited for: 3 -> 0; matrix products, arithmetic and copies ran while one was open for 1% -> 10% of each run, Pallas kernels for 0% -> 45%
where the time goes in v1:
time: 137 us; the launch traced here: 136 us
  Pallas kernels  92.2 us (67%)
  local copies, waits for them, and re-layouts  15.8 us (12%)
  between operations  14.8 us (11%)
  blocking collectives  11.9 us (9%)
    pallas_call x1, Pallas kernels, image_rows(): pl.pallas_call(functools.partial(image_kernel, n), out_shape=jax.ShapeDty...  61.2 us
    pallas_call x1, Pallas kernels, attention(): pl.pallas_call(functools.partial(attend_kernel, n, span, width), grid=(KV...  31.1 us
    unnamed x22, local copies, waits for them, and re-layouts  12.7 us
    unnamed x1, blocking collectives  11.9 us
  transfers between devices with their start and end apart: 1, of which 0 were waited for; matrix products, arithmetic and copies ran while one was open for 10% of the time, Pallas kernels for 45%

profile of v1, /device:TPU:1, one launch (start us, length us, event | category | flops | bytes accessed | tf_op | source)
XLA Modules:
  0.0 136.3 jit_solution(1780600122186501287)
XLA Ops:
  6.5 0.0 copy-start.8
  6.5 0.0 copy-start.4
  6.5 0.0 copy-start.5
  6.5 0.0 copy-start.6
  6.5 0.0 copy-start.7
  6.5 0.0 all-gather.2.cloned.1.call-start
  6.6 0.7 all-gather.2.cloned.1.call-update
  7.3 1.2 dynamic_slice.4
  9.2 8.7 %copy.14.fc1_hbm = bf16[3200,800]{1,0:T(8,128)(2,1)} copy(bf16[3200,800]{0,1:T(8,128)(2,1)} %param.15) | data formatting | bytes 10240000 | tf_op args[2]
  17.9 0.0 copy-done.4
  17.9 0.6 reshape.22.proj_gain
  18.5 0.0 copy-done.5
  18.5 0.6 reshape.23.proj_bias
  19.1 0.0 copy-done.6
  19.1 0.6 reshape.21.vit_gain
  19.7 0.0 copy-done.8
  19.7 0.6 dynamic-slice
  21.0 0.0 copy-done.7
  21.0 0.2 dynamic-update-slice
  21.3 11.9 %all-reduce = s32[1024]{0:T(1024)S(1)} all-reduce(s32[1024]{0:T(1024)S(1)} %dynamic-update-slice), channel_id=1, replica_groups=mesh['groups'=2,'ctx'=16] {'ctx'}, use_global_device_ids=true, to_apply=%add | all-reduce | flops 1024 | bytes 8192
  33.2 0.1 fusion.2
  33.2 0.1 fusion
  33.3 0.1 maximum_bitcast_fusion
  33.4 0.1 maximum_bitcast_fusion.1
  33.4 0.6 pad_maximum_fusion.turn
  34.0 0.0 copy-start.2
  34.0 0.0 copy-start.3
  34.0 61.2 %shard_map.127.iq.ik.iv = bf16[16,10240]{1,0:T(8,128)(2,1)} custom-call(bf16[4,3200]{1,0:T(4,128)(2,1)} %patches.1, f32[1,3200]{1,0:T(1,128)} %reshape.21.vit_gain, bf16[3200,800]{1,0:T(8,128)(2,1)} %copy.14.fc1_hbm, bf16[800,3200]{1,0:T(8,128)(2,1)} %fc2_hbm.1, f32[4,3200]{1,0:T(4,128)} %reshape.22.proj_gain, f32[4,3200]{1,0:T(4,128)} %reshape.23.proj_bias, ...), custom_call_target="tpu_custom_call" | custom-call | flops 1082654720 | bytes 33832960 | tf_op jit(solution)/shard_map/pallas_call | solution.py:276
  95.2 0.0 all-gather.2.cloned.1.call-done.keys.vals
  95.2 0.0 copy-done.2
  95.2 0.0 copy-done.3
  95.2 0.0 copy-start
  95.3 2.2 %copy-done = bf16[1024,2048]{1,0:T(8,128)(2,1)S(1)} copy-done((bf16[1024,2048]{1,0:T(8,128)(2,1)S(1)}, bf16[1024,2048]{1,0:T(8,128)(2,1)}, u32[]{:S(2)}) %copy-start) | copy-done | bytes 4194328
  97.4 0.0 copy-start.1
  97.4 1.0 copy-done.1
  98.4 31.1 %shard_map.128 = bf16[64,8192]{1,0:T(8,128)(2,1)} custom-call(bf16[64,8192]{1,0:T(8,128)(2,1)S(1)} %copy-done.2, bf16[1024,2048]{1,0:T(8,128)(2,1)S(1)} %copy-done, bf16[1024,2048]{1,0:T(8,128)(2,1)S(1)} %copy-done, s32[1,1024]{1,0:T(1,128)S(1)} %bitcast.9, s32[1,16]{1,0:T(1,128)S(1)} %bitcast.10, bf16[16,10240]{1,0:T(8,128)(2,1)S(1)} %copy-done.1, ...), custom_call_target="tpu_custom_call" | custom-call | flops 1610612736 | bytes 6291456 | tf_op jit(solution)/shard_map/pallas_call | solution.py:361
  (1 shorter events, 0.0 us)
Async XLA Ops:
  6.5 13.2 %copy-start.8 = (u32[32]{0:T(128)S(1)}, u32[32]{0:T(128)}, u32[]{:S(2)}) copy-start(u32[32]{0:T(128)} %constant.20) | copy-start | bytes 388
  6.5 11.3 %copy-start.4 = (f32[12800]{0:T(1024)S(1)}, f32[12800]{0:T(1024)}, u32[]{:S(2)}) copy-start(f32[12800]{0:T(1024)} %param.17) | copy-start | bytes 153604
  6.5 12.0 %copy-start.5 = (f32[12800]{0:T(1024)S(1)}, f32[12800]{0:T(1024)}, u32[]{:S(2)}) copy-start(f32[12800]{0:T(1024)} %param.18) | copy-start | bytes 153604
  6.5 12.6 %copy-start.6 = (f32[3200]{0:T(1024)S(1)}, f32[3200]{0:T(1024)}, u32[]{:S(2)}) copy-start(f32[3200]{0:T(1024)} %param.14) | copy-start | bytes 38404
  6.5 14.5 %copy-start.7 = (s32[64]{0:T(128)S(1)}, s32[64]{0:T(128)}, u32[]{:S(2)}) copy-start(s32[64]{0:T(128)} %param.24) | copy-start | bytes 772
  6.5 88.7 %all-gather.2.cloned.1.call-start = ((), (), s32[]{:S(2)}) async-start(), calls=%async_computation | async-start | bytes 4456448 | tf_op jit(solution)/shard_map/all_gather | solution.py:406
  34.0 61.2 %copy-start.2 = (bf16[64,8192]{1,0:T(8,128)(2,1)S(1)}, bf16[64,8192]{1,0:T(8,128)(2,1)}, u32[]{:S(2)}) copy-start(bf16[64,8192]{1,0:T(8,128)(2,1)} %query.1) | copy-start | bytes 3145732
  34.0 61.2 %copy-start.3 = (s32[16]{0:T(128)S(1)}, s32[16]{0:T(128)}, u32[]{:S(2)}) copy-start(s32[16]{0:T(128)} %param.25) | copy-start | bytes 196
  95.2 2.2 %copy-start = (bf16[1024,2048]{1,0:T(8,128)(2,1)S(1)}, bf16[1024,2048]{1,0:T(8,128)(2,1)}, u32[]{:S(2)}) copy-start(bf16[1024,2048]{1,0:T(8,128)(2,1)} %all-gather.2.cloned.1.call-done.keys.vals) | copy-start | bytes 12582916
  97.4 1.0 copy-start.1
Sparse Core Ops, SparseCore 0:
  9.5 59.4 all-gather.1

commit v2 on v1

--- a/solution.py
+++ b/solution.py
@@ -49,7 +49,9 @@
     llm_gain,
     qkv_hbm,
     turn,
+    doc,
     out,
+    doc_out,
     fc1,
     fc2,
     proj,
@@ -180,10 +182,17 @@
 
     values = patches[...].astype(F32)
     mean_sq = jnp.mean(values * values, axis=-1, keepdims=True)
-    g1[slot] = (values * lax.rsqrt(mean_sq + 1e-6) * vit_gain[...]).astype(BF16)
+    g1[slot, :, pl.ds(DV, EXT)] = doc[...]
+    g1[slot, :, pl.ds(0, DV)] = (values * lax.rsqrt(mean_sq + 1e-6) * vit_gain[...]).astype(BF16)
     sends = gather(g1, 0)
 
-    unpack(g1, DV)
+    unpack(g1, DV + EXT)
+    lane = lax.broadcasted_iota(jnp.int32, (1, 128), 1)
+    for m in range(n // 2):
+        low, high = [
+            work[DV // 128, pl.ds(4 * (((i % 2) * 2 + (i // 2) % 2) * Z + i // 4), 1), :]
+            for i in (2 * m, 2 * m + 1)]
+        doc_out[:, pl.ds(m * 128, 128)] = jnp.where(lane < 64, low, pltpu.roll(high, 64, 1))
     for j in range(DV // 128):
         lhs[:, pl.ds(j * 128, 128)] = work[j].astype(BF16)
     loads[0].wait()
@@ -192,7 +201,8 @@
     @pl.loop(0, DV // 640)
     def _(j):
         at = pl.ds(pl.multiple_of(j * 640, 128), 640)
-        hid_acc[...] += jnp.dot(lhs[:, at], fc1[at, :], preferred_element_type=F32)
+        hid_acc[...] += lax.dot_general(
+            lhs[:, at], fc1[:, at], (((1,), (1,)), ((), ())), preferred_element_type=F32)
 
     hidden[...] = gelu(hid_acc[...]).astype(BF16)
     loads[1].wait()
@@ -259,7 +269,7 @@
         copy.wait_send()
 
 
-def image_rows(n, patches, vit_gain, fc1, fc2, proj_gain, proj_bias, proj, llm_gain, qkv, turn):
+def image_rows(n, patches, vit_gain, fc1, fc2, proj_gain, proj_bias, proj, llm_gain, qkv, turn, doc):
     Z = n // 4
     vm = pl.BlockSpec(memory_space=pltpu.VMEM)
     hbm = pl.BlockSpec(memory_space=pl.ANY)
@@ -270,24 +280,27 @@
             pltpu.VMEM((2, Z, SHUF, width), BF16),
         ] + [pltpu.VMEM((Z, SHUF, width), BF16)] * 4
 
-    hid = fc1.shape[1]
+    hid = fc1.shape[0]
     cols = proj.shape[1]
     weights = sum(w.size for w in (fc1, fc2, proj, qkv))
     return pl.pallas_call(
         functools.partial(image_kernel, n),
-        out_shape=jax.ShapeDtypeStruct((n, SHUF * ROWW), BF16),
-        in_specs=[vm, vm, hbm, hbm, vm, vm, hbm, vm, hbm, vm],
-        out_specs=vm,
+        out_shape=(
+            jax.ShapeDtypeStruct((n, SHUF * ROWW), BF16),
+            jax.ShapeDtypeStruct((1, n * HD // 2), F32),
+        ),
+        in_specs=[vm, vm, hbm, hbm, vm, vm, hbm, vm, hbm, vm, vm],
+        out_specs=(vm, vm),
         scratch_shapes=[
             pltpu.VMEM(fc1.shape, BF16),
             pltpu.VMEM(fc2.shape, BF16),
             pltpu.VMEM(proj.shape, BF16),
             pltpu.VMEM(qkv.shape, BF16),
-            pltpu.VMEM((n, SHUF, DV), BF16),
+            pltpu.VMEM((n, SHUF, DV + EXT), BF16),
             pltpu.VMEM((n, SHUF, DV), BF16),
             pltpu.VMEM((n, SHUF, ROWW), BF16),
         ] + reduce_bufs(DV) + reduce_bufs(ROWW + EXT) + [
-            pltpu.VMEM((DV // 128, n * SHUF, 128), F32),
+            pltpu.VMEM((DV // 128 + 1, n * SHUF, 128), F32),
             pltpu.VMEM((n * SHUF, DV), BF16),
             pltpu.VMEM((n * SHUF, hid), F32),
             pltpu.VMEM((n * SHUF, hid), BF16),
@@ -302,7 +315,7 @@
             collective_id=0, has_side_effects=True, vmem_limit_bytes=56 * 2 ** 20),
         cost_estimate=pl.CostEstimate(
             flops=64 * weights, bytes_accessed=2 * weights, transcendentals=0),
-    )(patches, vit_gain, fc1, fc2, proj_gain, proj_bias, proj, llm_gain, qkv, turn)
+    )(patches, vit_gain, fc1, fc2, proj_gain, proj_bias, proj, llm_gain, qkv, turn, doc)
 
 
 def attend_kernel(n, span, width, query, keys, vals, doc, pos, iq, ik, iv, out, bias, hit_k, img_k, hit_q, img_q):
@@ -317,7 +330,7 @@
         docs = doc[...]
         q_pos = me * rows + lax.broadcasted_iota(jnp.int32, (rows, docs.shape[1]), 0)
         k_pos = lax.broadcasted_iota(jnp.int32, (rows, docs.shape[1]), 1)
-        q_doc = jnp.sum(jnp.where(q_pos == k_pos, docs, 0), axis=1, keepdims=True)
+        q_doc = jnp.sum(jnp.where(q_pos == k_pos, docs, 0.0), axis=1, keepdims=True)
         k_doc = doc[:, pl.ds(first, width)]
         ok = (first + k_pos[:, :width] <= q_pos[:, :width]) & (k_doc == q_doc)
         bias[...] = jnp.where(ok, 0.0, -1e30)
@@ -341,15 +354,18 @@
     k = put(img_k[...], hit_k[...], ik[...], keys[pl.ds(first, width), :])
     v = put(img_k[...], hit_k[...], iv[...], vals[pl.ds(first, width), :])
     scale = HD ** -0.5
-    for m in range(group):
-        at = slice(m * HD, (m + 1) * HD)
-        q = put(img_q[...], hit_q[...], iq[:, at], query[:, at])
+    table = jnp.concatenate([bias[...]] * 4, axis=0)
+    for m in range(0, group, 4):
+        heads = [slice((m + i) * HD, (m + i + 1) * HD) for i in range(4)]
+        q = jnp.concatenate(
+            [put(img_q[...], hit_q[...], iq[:, at], query[:, at]) for at in heads], axis=0)
         s = lax.dot_general(q, k, (((1,), (1,)), ((), ())), preferred_element_type=F32)
-        s = s * scale + bias[...]
+        s = s * scale + table
         w = jnp.exp(s - jnp.max(s, axis=1, keepdims=True))
         total = jnp.sum(w, axis=1, keepdims=True)
-        o = jnp.dot(w.astype(BF16), v, preferred_element_type=F32)
-        out[:, at] = (o / total).astype(BF16)
+        o = (jnp.dot(w.astype(BF16), v, preferred_element_type=F32) / total).astype(BF16)
+        for i in range(4):
+            out[:, heads[i]] = o[i * rows:(i + 1) * rows]
 
 
 def attention(n, query, keyvalue, doc, pos, image):
@@ -404,19 +420,19 @@
     image_positions,
 ):
     kv_all = lax.all_gather(text_keyvalue, "ctx", axis=0, tiled=True)
-    doc_all = lax.all_gather(doc_ids, "ctx", axis=0, tiled=True)
+    doc = jnp.pad(doc_ids.astype(BF16)[None, :], ((0, SHUF - 1), (0, HD - doc_ids.shape[0])))
     half = HD // 2
     inv_freq = 1000000.0 ** (-2.0 * jnp.arange(half, dtype=F32) / HD)
     own_pos = lax.dynamic_index_in_dim(image_positions, lax.axis_index("ctx"), 0, keepdims=False)
     angle = own_pos.astype(F32) * inv_freq
     cosine, sine = jnp.cos(angle), jnp.sin(angle)
     turn = jnp.stack([jnp.concatenate([cosine, cosine]), jnp.concatenate([-sine, sine])])
-    image = image_rows(
-        n, patches, vit_gain.reshape(1, DV), vit_fc1, vit_fc2,
+    image, doc_all = image_rows(
+        n, patches, vit_gain.reshape(1, DV), vit_fc1.T, vit_fc2,
         proj_gain.reshape(SHUF, DV), proj_bias.reshape(SHUF, DV), proj_weight,
-        llm_gain.reshape(1, -1), qkv_weight, turn)
+        llm_gain.reshape(1, -1), qkv_weight, turn, doc)
     return attention(
-        n, text_query, kv_all, doc_all.reshape(1, -1), image_positions.reshape(1, -1), image)
+        n, text_query, kv_all, doc_all, image_positions.reshape(1, -1), image)
 
 
 def solution(mesh):

time: 137 us -> 105 us (0.77)
  Pallas kernels: 92.2 us -> 78.6 us
  blocking collectives: 11.9 us -> 0 us
  local copies, waits for them, and re-layouts: 15.8 us -> 9.87 us
    pallas_call x1, Pallas kernels: 31.1 us -> 14.2 us  [attention(): pl.pallas_call(functools.partial(attend_kernel, n, span, width), grid=(KV...]
    unnamed x1 -> x0, blocking collectives: 11.9 us -> none
    unnamed x22 -> x10, local copies, waits for them, and re-layouts: 12.7 us -> 3.84 us
    pallas_call x1, Pallas kernels: 61.2 us -> 64.4 us  [image_rows(): pl.pallas_call(functools.partial(image_kernel, n), out_shape=(jax.ShapeDt...]
  transfers between devices with their start and end apart: 1 -> 1, of which waited for: 0 -> 0; matrix products, arithmetic and copies ran while one was open for 10% -> 7% of each run, Pallas kernels for 45% -> 61%
where the time goes in v2:
time: 105 us
  Pallas kernels  78.6 us (75%)
  between operations  14.1 us (13%)
  local copies, waits for them, and re-layouts  9.87 us (9%)
  other arithmetic  1.47 us (1%)
    pallas_call x1, Pallas kernels, image_rows(): pl.pallas_call(functools.partial(image_kernel, n), out_shape=(jax.ShapeDt...  64.4 us
    pallas_call x1, Pallas kernels, attention(): pl.pallas_call(functools.partial(attend_kernel, n, span, width), grid=(KV...  14.2 us
    unnamed x10, local copies, waits for them, and re-layouts  3.84 us
  transfers between devices with their start and end apart: 1, of which 0 were waited for; matrix products, arithmetic and copies ran while one was open for 7% of the time, Pallas kernels for 61%

profile of v2, /device:TPU:1, one launch (start us, length us, event | category | flops | bytes accessed | tf_op | source)
XLA Modules:
  0.0 104.8 jit_solution(15691594244228705830)
XLA Ops:
  6.5 0.0 all-gather.2.cloned.1.call-start
  6.5 0.7 all-gather.2.cloned.1.call-update
  7.3 1.2 %dynamic_slice.4 = s32[1]{0:T(128)} dynamic-slice(s32[16]{0:T(128)} %param.25, s32[]{:T(128)S(6)} %select_n.4), dynamic_slice_sizes={1} | dynamic-slice | bytes 12 | tf_op jit(solution)/shard_map/jit(dynamic_index_in_dim)/dynamic_slice | solution.py:426
  9.2 1.3 %reshape.16.vit_gain = f32[1,3200]{1,0:T(1,128)} reshape(f32[3200]{0:T(1024)} %param.14) | data formatting | bytes 25600 | tf_op jit(solution)/shard_map/reshape | solution.py:431
  10.5 1.4 %reshape.17.proj_gain = f32[4,3200]{1,0:T(4,128)} reshape(f32[12800]{0:T(1024)} %param.17) | data formatting | bytes 102400 | tf_op jit(solution)/shard_map/reshape | solution.py:432
  11.9 1.4 %reshape.18.proj_bias = f32[4,3200]{1,0:T(4,128)} reshape(f32[12800]{0:T(1024)} %param.18) | data formatting | bytes 102400 | tf_op jit(solution)/shard_map/reshape | solution.py:432
  13.4 0.7 convert_bitcast_fusion
  14.0 0.6 pad.4.doc
  14.6 0.1 fusion.2
  14.7 0.1 fusion
  14.7 0.1 maximum_bitcast_fusion
  14.8 0.1 maximum_bitcast_fusion.1
  14.9 0.6 pad_maximum_fusion.turn
  15.4 0.0 copy-start.2
  15.4 0.0 copy-start.4
  15.4 64.4 %shard_map.127 = (bf16[16,10240]{1,0:T(8,128)(2,1)}, f32[1,1024]{1,0:T(1,128)}) custom-call(bf16[4,3200]{1,0:T(4,128)(2,1)} %patches.1, f32[1,3200]{1,0:T(1,128)} %reshape.16.vit_gain, bf16[800,3200]{1,0:T(8,128)(2,1)} %bitcast.11, bf16[800,3200]{1,0:T(8,128)(2,1)} %fc2_hbm.1, f32[4,3200]{1,0:T(4,128)} %reshape.17.proj_gain, f32[4,3200]{1,0:T(4,128)} %reshape.18.proj_bias, ...), custom_call_target="tpu_custom_call" | custom-call | flops 1082654720 | bytes 33832960 | tf_op jit(solution)/shard_map/pallas_call | solution.py:286
  79.8 0.0 all-gather.2.cloned.1.call-done.keys.vals
  79.9 0.0 copy-done.2
  79.9 0.0 copy-done.4
  79.9 0.0 copy-start
  79.9 2.2 %copy-done = bf16[1024,2048]{1,0:T(8,128)(2,1)S(1)} copy-done((bf16[1024,2048]{1,0:T(8,128)(2,1)S(1)}, bf16[1024,2048]{1,0:T(8,128)(2,1)}, u32[]{:S(2)}) %copy-start) | copy-done | bytes 4194328
  82.1 0.0 copy-start.1
  82.1 1.0 copy-done.1
  83.0 0.0 copy-start.3
  83.0 0.7 copy-done.3
  83.7 14.2 %shard_map.128 = bf16[64,8192]{1,0:T(8,128)(2,1)} custom-call(bf16[64,8192]{1,0:T(8,128)(2,1)S(1)} %copy-done.2, bf16[1024,2048]{1,0:T(8,128)(2,1)S(1)} %copy-done, bf16[1024,2048]{1,0:T(8,128)(2,1)S(1)} %copy-done, f32[1,1024]{1,0:T(1,128)S(1)} %copy-done.3, s32[1,16]{1,0:T(1,128)S(1)} %bitcast.10, bf16[16,10240]{1,0:T(8,128)(2,1)S(1)} %copy-done.1, ...), custom_call_target="tpu_custom_call" | custom-call | flops 1610612736 | bytes 6291456 | tf_op jit(solution)/shard_map/pallas_call | solution.py:377
Async XLA Ops:
  6.5 73.3 %all-gather.2.cloned.1.call-start = ((), (), s32[]{:S(2)}) async-start(), calls=%async_computation | async-start | bytes 4456448 | tf_op jit(solution)/shard_map/all_gather | solution.py:422
  15.4 64.4 %copy-start.2 = (bf16[64,8192]{1,0:T(8,128)(2,1)S(1)}, bf16[64,8192]{1,0:T(8,128)(2,1)}, u32[]{:S(2)}) copy-start(bf16[64,8192]{1,0:T(8,128)(2,1)} %query.1) | copy-start | bytes 3145732
  15.4 64.4 %copy-start.4 = (s32[16]{0:T(128)S(1)}, s32[16]{0:T(128)}, u32[]{:S(2)}) copy-start(s32[16]{0:T(128)} %param.25) | copy-start | bytes 196
  79.9 2.2 %copy-start = (bf16[1024,2048]{1,0:T(8,128)(2,1)S(1)}, bf16[1024,2048]{1,0:T(8,128)(2,1)}, u32[]{:S(2)}) copy-start(bf16[1024,2048]{1,0:T(8,128)(2,1)} %all-gather.2.cloned.1.call-done.keys.vals) | copy-start | bytes 12582916
  82.1 1.0 copy-start.1
  83.0 0.7 copy-start.3
Sparse Core Ops, SparseCore 0:
  9.5 56.2 all-gather.1

commit v3 on v2

--- a/solution.py
+++ b/solution.py
@@ -48,7 +48,8 @@
     proj_hbm,
     llm_gain,
     qkv_hbm,
-    turn,
+    cosine,
+    sine,
     doc,
     out,
     doc_out,
@@ -76,8 +77,19 @@
     def dev(zz, yy, cc):
         return (group, zz * 4 + yy * 2 + cc)
 
-    zs = [lax.rem(z + k, Z) for k in range(Z)]
-    zr = [lax.rem(z + Z - k, Z) for k in range(Z)]
+    if Z & (Z - 1):
+        zs = [lax.rem(z + k, Z) for k in range(Z)]
+        zr = [lax.rem(z + Z - k, Z) for k in range(Z)]
+    else:
+
+        def flipped(k):
+            at = z
+            for b in range(k.bit_length()):
+                if (k >> b) & 1:
+                    at = at + 2 ** b - 2 ** (b + 1) * lax.rem(z // 2 ** b, 2)
+            return at
+
+        zs = zr = [flipped(k) for k in range(Z)]
     ydev, cdev = dev(z, 1 - y, c), dev(z, y, 1 - c)
     own = (c * 2 + y) * Z
     own_y = (c * 2 + 1 - y) * Z
@@ -182,8 +194,13 @@
 
     values = patches[...].astype(F32)
     mean_sq = jnp.mean(values * values, axis=-1, keepdims=True)
-    g1[slot, :, pl.ds(DV, EXT)] = doc[...]
-    g1[slot, :, pl.ds(0, DV)] = (values * lax.rsqrt(mean_sq + 1e-6) * vit_gain[...]).astype(BF16)
+    g1[slot, :, pl.ds(DV, EXT)] = jnp.zeros((SHUF, EXT), BF16)
+    g1[slot, :, pl.ds(DV, doc.shape[1])] = jnp.broadcast_to(
+        doc[...].astype(F32), (SHUF, doc.shape[1])).astype(BF16)
+    normed = values * lax.rsqrt(mean_sq + 1e-6)
+    for j in range(DV // 128):
+        g1[slot, :, pl.ds(j * 128, 128)] = (
+            normed[:, j * 128:(j + 1) * 128] * vit_gain[j:j + 1, :]).astype(BF16)
     sends = gather(g1, 0)
 
     unpack(g1, DV + EXT)
@@ -221,7 +238,11 @@
     row_mean = jnp.sum(jnp.sum(shuffled, axis=1, keepdims=True), axis=0, keepdims=True) / (SHUF * DV)
     centre = shuffled - row_mean
     var = jnp.sum(jnp.sum(centre * centre, axis=1, keepdims=True), axis=0, keepdims=True) / (SHUF * DV)
-    g2[slot] = (centre * lax.rsqrt(var + 1e-5) * proj_gain[...] + proj_bias[...]).astype(BF16)
+    normed = centre * lax.rsqrt(var + 1e-5)
+    for j in range(DV // 128):
+        at = pl.ds(j, SHUF, stride=DV // 128)
+        g2[slot, :, pl.ds(j * 128, 128)] = (
+            normed[:, j * 128:(j + 1) * 128] * proj_gain[at, :] + proj_bias[at, :]).astype(BF16)
     sends += gather(g2, 1)
 
     unpack(g2, DV)
@@ -253,7 +274,7 @@
     sends += more
     square_sum = jnp.sum(total[:, ROWW:], axis=1, keepdims=True)
     inv_rms = lax.rsqrt(square_sum / D + 1e-6)
-    cosine, sine = turn[0:1, :], turn[1:2, :]
+    cosine, sine = cosine[...], sine[...]
     row = lax.broadcasted_iota(jnp.int32, (SHUF, HD), 0)
     for h in range(ROWW // HD):
         x = total[:, h * HD:(h + 1) * HD] * inv_rms
@@ -269,7 +290,7 @@
         copy.wait_send()
 
 
-def image_rows(n, patches, vit_gain, fc1, fc2, proj_gain, proj_bias, proj, llm_gain, qkv, turn, doc):
+def image_rows(n, patches, vit_gain, fc1, fc2, proj_gain, proj_bias, proj, llm_gain, qkv, cosine, sine, doc):
     Z = n // 4
     vm = pl.BlockSpec(memory_space=pltpu.VMEM)
     hbm = pl.BlockSpec(memory_space=pl.ANY)
@@ -289,7 +310,7 @@
             jax.ShapeDtypeStruct((n, SHUF * ROWW), BF16),
             jax.ShapeDtypeStruct((1, n * HD // 2), F32),
         ),
-        in_specs=[vm, vm, hbm, hbm, vm, vm, hbm, vm, hbm, vm, vm],
+        in_specs=[vm, vm, hbm, hbm, vm, vm, hbm, vm, hbm, vm, vm, vm],
         out_specs=(vm, vm),
         scratch_shapes=[
             pltpu.VMEM(fc1.shape, BF16),
@@ -315,7 +336,7 @@
             collective_id=0, has_side_effects=True, vmem_limit_bytes=56 * 2 ** 20),
         cost_estimate=pl.CostEstimate(
             flops=64 * weights, bytes_accessed=2 * weights, transcendentals=0),
-    )(patches, vit_gain, fc1, fc2, proj_gain, proj_bias, proj, llm_gain, qkv, turn, doc)
+    )(patches, vit_gain, fc1, fc2, proj_gain, proj_bias, proj, llm_gain, qkv, cosine, sine, doc)
 
 
 def attend_kernel(n, span, width, query, keys, vals, doc, pos, iq, ik, iv, out, bias, hit_k, img_k, hit_q, img_q):
@@ -353,15 +374,15 @@
 
     k = put(img_k[...], hit_k[...], ik[...], keys[pl.ds(first, width), :])
     v = put(img_k[...], hit_k[...], iv[...], vals[pl.ds(first, width), :])
-    scale = HD ** -0.5
+    scale = HD ** -0.5 * 1.4426950408889634
     table = jnp.concatenate([bias[...]] * 4, axis=0)
     for m in range(0, group, 4):
         heads = [slice((m + i) * HD, (m + i + 1) * HD) for i in range(4)]
         q = jnp.concatenate(
             [put(img_q[...], hit_q[...], iq[:, at], query[:, at]) for at in heads], axis=0)
         s = lax.dot_general(q, k, (((1,), (1,)), ((), ())), preferred_element_type=F32)
-        s = s * scale + table
-        w = jnp.exp(s - jnp.max(s, axis=1, keepdims=True))
+        s = s + table
+        w = jnp.exp2((s - jnp.max(s, axis=1, keepdims=True)) * scale)
         total = jnp.sum(w, axis=1, keepdims=True)
         o = (jnp.dot(w.astype(BF16), v, preferred_element_type=F32) / total).astype(BF16)
         for i in range(4):
@@ -396,7 +417,7 @@
             pltpu.VMEM((rows, n), BF16),
             pltpu.VMEM((rows, HD), F32),
         ],
-        compiler_params=pltpu.CompilerParams(vmem_limit_bytes=48 * 2 ** 20),
+        compiler_params=pltpu.CompilerParams(vmem_limit_bytes=60 * 2 ** 20),
         cost_estimate=pl.CostEstimate(
             flops=4 * rows * QH * HD * width, bytes_accessed=4 * query.size + 2 * keyvalue.size,
             transcendentals=rows * QH * width),
@@ -420,17 +441,17 @@
     image_positions,
 ):
     kv_all = lax.all_gather(text_keyvalue, "ctx", axis=0, tiled=True)
-    doc = jnp.pad(doc_ids.astype(BF16)[None, :], ((0, SHUF - 1), (0, HD - doc_ids.shape[0])))
+    doc = doc_ids.reshape(1, -1)
     half = HD // 2
-    inv_freq = 1000000.0 ** (-2.0 * jnp.arange(half, dtype=F32) / HD)
+    lane = lax.broadcasted_iota(jnp.int32, (1, HD), 1)
+    inv_freq = 1000000.0 ** (-2.0 * (lane % half).astype(F32) / HD)
     own_pos = lax.dynamic_index_in_dim(image_positions, lax.axis_index("ctx"), 0, keepdims=False)
     angle = own_pos.astype(F32) * inv_freq
-    cosine, sine = jnp.cos(angle), jnp.sin(angle)
-    turn = jnp.stack([jnp.concatenate([cosine, cosine]), jnp.concatenate([-sine, sine])])
+    cosine, sine = jnp.cos(angle), jnp.where(lane < half, -jnp.sin(angle), jnp.sin(angle))
     image, doc_all = image_rows(
-        n, patches, vit_gain.reshape(1, DV), vit_fc1.T, vit_fc2,
-        proj_gain.reshape(SHUF, DV), proj_bias.reshape(SHUF, DV), proj_weight,
-        llm_gain.reshape(1, -1), qkv_weight, turn, doc)
+        n, patches, vit_gain.reshape(-1, 128), vit_fc1.T, vit_fc2,
+        proj_gain.reshape(-1, 128), proj_bias.reshape(-1, 128), proj_weight,
+        llm_gain.reshape(1, -1), qkv_weight, cosine, sine, doc)
     return attention(
         n, text_query, kv_all, doc_all, image_positions.reshape(1, -1), image)
 

time: 105 us -> 93 us (0.89)
  local copies, waits for them, and re-layouts: 9.87 us -> 1.24 us
  Pallas kernels: 78.6 us -> 76.1 us
    reshape x3 -> x0, local copies, waits for them, and re-layouts: 4.22 us -> none  [the longest x1 1.45 us: shards(): proj_gain.reshape(SHUF, DV)]
    unnamed x10 -> x0, local copies, waits for them, and re-layouts: 3.84 us -> none
    pallas_call x1, Pallas kernels: 64.4 us -> 62.1 us  [image_rows(): pl.pallas_call(functools.partial(image_kernel, n), out_shape=(jax.ShapeDt...]
  transfers between devices with their start and end apart: 1 -> 1, of which waited for: 0 -> 0; matrix products, arithmetic and copies ran while one was open for 7% -> 2% of each run, Pallas kernels for 61% -> 67%
where the time goes in v3:
time: 93 us; the launch traced here: 92.8 us
  Pallas kernels  76.1 us (82%)
  between operations  14.1 us (15%)
  local copies, waits for them, and re-layouts  1.24 us (1%)
    pallas_call x1, Pallas kernels, image_rows(): pl.pallas_call(functools.partial(image_kernel, n), out_shape=(jax.ShapeDt...  62.1 us
    pallas_call x1, Pallas kernels, attention(): pl.pallas_call(functools.partial(attend_kernel, n, span, width), grid=(KV...  14.1 us
  transfers between devices with their start and end apart: 1, of which 0 were waited for; matrix products, arithmetic and copies ran while one was open for 2% of the time, Pallas kernels for 67%

profile of v3, /device:TPU:1, one launch (start us, length us, event | category | flops | bytes accessed | tf_op | source)
XLA Modules:
  0.0 92.8 jit_solution(7779786589521778720)
XLA Ops:
  6.5 0.0 all-gather.2.cloned.1.call-start
  6.5 0.7 all-gather.2.cloned.1.call-update
  7.3 1.2 %dynamic_slice.4 = s32[1]{0:T(128)} dynamic-slice(s32[16]{0:T(128)} %param.25, s32[]{:T(128)S(6)} %select_n.27), dynamic_slice_sizes={1} | dynamic-slice | bytes 12 | tf_op jit(solution)/shard_map/jit(dynamic_index_in_dim)/dynamic_slice | solution.py:448
  9.2 0.6 compare_select_fusion
  9.7 62.1 %shard_map.127 = (bf16[16,10240]{1,0:T(8,128)(2,1)}, f32[1,1024]{1,0:T(1,128)}) custom-call(bf16[4,3200]{1,0:T(4,128)(2,1)} %patches.1, f32[25,128]{1,0:T(8,128)} %bitcast.11, bf16[800,3200]{1,0:T(8,128)(2,1)} %bitcast.8, bf16[800,3200]{1,0:T(8,128)(2,1)} %fc2_hbm.1, f32[100,128]{1,0:T(8,128)} %bitcast.9, f32[100,128]{1,0:T(8,128)} %bitcast.10, ...), custom_call_target="tpu_custom_call" | custom-call | flops 1082654720 | bytes 33832960 | tf_op jit(solution)/shard_map/pallas_call | solution.py:307
  71.8 0.0 all-gather.2.cloned.1.call-done.keys.vals
  71.9 14.1 %shard_map.128 = bf16[64,8192]{1,0:T(8,128)(2,1)} custom-call(bf16[64,8192]{1,0:T(8,128)(2,1)} %query.1, bf16[1024,2048]{1,0:T(8,128)(2,1)} %all-gather.2.cloned.1.call-done.keys.vals, bf16[1024,2048]{1,0:T(8,128)(2,1)} %all-gather.2.cloned.1.call-done.keys.vals, f32[1,1024]{1,0:T(1,128)} %get-tuple-element.7.doc, s32[1,16]{1,0:T(1,128)} %bitcast.13, ...), custom_call_target="tpu_custom_call" | custom-call | flops 1610612736 | bytes 6291456 | tf_op jit(solution)/shard_map/pallas_call | solution.py:398
Async XLA Ops:
  6.5 65.3 %all-gather.2.cloned.1.call-start = ((), (), s32[]{:S(2)}) async-start(), calls=%async_computation | async-start | bytes 4456448 | tf_op jit(solution)/shard_map/all_gather | solution.py:443
Sparse Core Ops, SparseCore 0:
  9.5 58.3 all-gather.1
